TPU v7x, 32 devices: a whole 2x2x4 slice. The times are simulated.
32 devices in a mesh: seq: 8 (over y, x, core), dp: 4 (over z).
Axes of the slice: x: 2, y: 2, z: 4, core: 2. Of those that a mesh axis runs over, the one named last changes fastest.
Arguments:
- features: bfloat16 [8, 3072, 768], P('dp', 'seq'), may hold values from -32 to 32
- weight: bfloat16 [5, 768, 768], replicated, may hold values from -0.09375 to 0.09375
- cotangent: bfloat16 [8, 1536, 768], P('dp', 'seq'), may hold values from -6 to 6
Outputs:
- trunk_input: bfloat16 [8, 1536, 768], P('dp', None, 'seq')
- input_grad: bfloat16 [8, 3072, 768], P('dp', 'seq')
- weight_grad: float32 [5, 768, 768], P(None, 'dp', 'seq')
All inputs are finite; a program needn't handle non-finite values.
Results may differ from a plain program's by a relative error of at most 0.0027.
Values may be sent and summed in bfloat16 or wider, within the bound.
A program may use at most 128 MiB of HBM per device.

v0:
```python
import jax
import jax.numpy as jnp
from jax import lax
from jax.sharding import PartitionSpec as P

epsilon = 1e-06
root_half = 0.7071067811865476
inv_root_two_pi = 0.3989422804014327


def with_halo(block, sides, width):
    for axis, dim in sides:
        count = lax.axis_size(axis)
        forward = [(i, i + 1) for i in range(count - 1)]
        backward = [(target, source) for source, target in forward]
        low = lax.ppermute(
            lax.slice_in_dim(block, block.shape[dim] - width, None, axis=dim), axis, forward
        )
        high = lax.ppermute(lax.slice_in_dim(block, 0, width, axis=dim), axis, backward)
        block = jnp.concatenate([low, block, high], axis=dim)
    return block


def gaussian_unit(value):
    return 0.5 * value * (1.0 + jax.scipy.special.erf(value * root_half))


def gaussian_slope(value):
    return 0.5 * (
        1.0 + jax.scipy.special.erf(value * root_half)
    ) + value * inv_root_two_pi * jnp.exp(-0.5 * value * value)


def windows(padded, length, taps):
    return jnp.stack([padded[:, offset : offset + length] for offset in range(taps)], axis=2)


def shards(features, weight, cotangent):
    taps = weight.shape[0]
    channels = weight.shape[2]
    batch = features.shape[0]
    length = features.shape[1]
    reach = taps // 2
    floats = features.astype(jnp.float32)
    inverse = lax.rsqrt(jnp.mean(floats * floats, axis=-1, keepdims=True) + epsilon)
    normed = floats * inverse
    activations = gaussian_unit(normed).astype(jnp.bfloat16)
    halves = 0.5 * cotangent.astype(jnp.float32)
    upward = jnp.broadcast_to(halves[:, :, None, :], (batch, length // 2, 2, channels)).reshape(
        batch, length, channels
    )
    branch_grad = upward.astype(jnp.bfloat16)
    padded_acts = with_halo(activations, (("seq", 1),), reach)
    padded_grad = with_halo(branch_grad, (("seq", 1),), reach)
    window = windows(padded_acts, length, taps)
    mixed = jnp.einsum("blki,kio->blo", window, weight, preferred_element_type=jnp.float32)
    summed = floats + mixed
    paired = summed.reshape(batch, length // 2, 2, channels)
    pooled = (0.5 * (paired[:, :, 0] + paired[:, :, 1])).astype(jnp.bfloat16)
    trunk_input = lax.all_to_all(pooled, "seq", split_axis=2, concat_axis=1, tiled=True)
    grad_window = windows(padded_grad, length, taps)
    act_grad = jnp.einsum(
        "blko,kio->bli", grad_window, weight[::-1], preferred_element_type=jnp.float32
    )
    slope_grad = act_grad * gaussian_slope(normed)
    centred = jnp.mean(slope_grad * floats, axis=-1, keepdims=True)
    input_grad = (upward + inverse * slope_grad - floats * inverse**3 * centred).astype(
        jnp.bfloat16
    )
    sectioned = lax.psum_scatter(
        jnp.einsum("blo,blki->oki", branch_grad, window, preferred_element_type=jnp.float32),
        "seq",
        scatter_dimension=0,
        tiled=True,
    )
    finished = lax.psum_scatter(sectioned, "dp", scatter_dimension=2, tiled=True)
    weight_grad = jnp.transpose(finished, (1, 2, 0))
    return (trunk_input, input_grad, weight_grad)


def solution(mesh):
    return jax.shard_map(
        shards,
        mesh=mesh,
        in_specs=(P("dp", "seq", None), P(), P("dp", "seq", None)),
        out_specs=(P("dp", None, "seq"), P("dp", "seq", None), P(None, "dp", "seq")),
        check_vma=False,
    )
```

profile of v0, /device:TPU:0, one launch (start us, length us, event | category | flops | bytes accessed | tf_op | source)
XLA Modules:
  0.0 203.6 jit_solution(6358154660828981509)
XLA Ops:
  7.2 0.0 reduce-scatter.5.cloned.1.call-start
  7.2 2.0 fusion.50
  9.2 2.2 %broadcast_in_dim.4 = f32[2,192,2,768]{3,2,1,0:T(2,128)} broadcast(f32[2,192,768]{2,1,0:T(8,128)S(1)} %get-tuple-element.21), dimensions={0,1,3} | broadcast | bytes 3538944 | tf_op jit(solution)/shard_map/broadcast_in_dim | solution.py:49
  11.4 3.1 %reshape.47 = f32[2,384,768]{2,1,0:T(8,128)S(1)} reshape(f32[2,192,2,768]{3,2,1,0:T(2,128)} %broadcast_in_dim.4) | data formatting | bytes 4718592 | tf_op jit(solution)/shard_map/reshape | solution.py:49
  14.6 0.1 convert_element_type.39
  14.7 0.6 fusion.52
  15.3 2.3 %collective-permute-start.2 = (bf16[2,2,768]{2,1,0:T(2,128)(2,1)}, bf16[2,2,768]{2,1,0:T(2,128)(2,1)S(1)}, u32[]{:S(2)}, u32[]{:S(2)}) collective-permute-start(bf16[2,2,768]{2,1,0:T(2,128)(2,1)} %get-tuple-element.17), channel_id=1, source_target_pairs={{0,4},{4,8},{8,12},{12,16},{16,20},{20,24},{24,28},{1,5},{5,9},{9,... | collective-permute-start | bytes 18440 | tf_op jit(solution)/shard_map/ppermute | solution.py:16
  17.7 1.3 collective-permute-start.3
  19.0 0.3 fusion.17
  19.3 0.6 multiply_multiply_fusion
  19.9 1.6 broadcast_in_dim.5
  21.5 3.7 %convert_element_type.41 = bf16[2,384,1,768]{3,1,0,2:T(8,128)(2,1)} reshape(bf16[2,192,2,768]{3,2,1,0:T(2,128)(2,1)} %broadcast_in_dim.5) | data formatting | bytes 2359296 | tf_op jit(solution)/shard_map/convert_element_type | solution.py:52
  25.3 5.6 %rev.3 = bf16[5,768,768]{2,1,0:T(8,128)(2,1)} reverse(bf16[5,768,768]{2,1,0:T(8,128)(2,1)} %param.4), dimensions={0} | reverse | bytes 11796480 | tf_op jit(solution)/shard_map/rev | solution.py:63
  30.9 0.3 fusion.31
  31.1 0.3 fusion.41
  31.4 0.7 copy-done.3
  32.1 0.1 constant_dynamic-update-slice_fusion
  32.2 0.3 fusion.28
  32.5 0.3 fusion.39
  32.8 2.0 copy-done
  34.8 0.3 copy-done.2
  35.1 5.4 %fusion.21 = (f32[2,384]{1,0:T(2,128)S(1)}, f32[2,384,768]{2,1,0:T(8,128)S(1)}) fusion(bf16[2,384,768]{2,1,0:T(8,128)(2,1)S(1)} %copy-done.2, f32[2,384]{1,0:T(2,128)S(1)} %copy-done.7, bf16[2,384,5,768]{3,1,0,2:T(8,128)(2,1)S(1)} %fusion.39, bf16[5,768,768]{2,1,0:T(8,128)(2,1)S(1)} %copy-done), kind=kOutput, calls=%fused_computation.27 | convolution fusion | flops 4537515008 | bytes 15341568 | tf_op jit(solution)/shard_map/blko,kio->bli/dot_general | solution.py:62
  40.6 2.0 fusion.20
  42.6 5.1 %collective-permute-start = (bf16[2,2,768]{2,1,0:T(2,128)(2,1)S(1)}, bf16[2,2,768]{2,1,0:T(2,128)(2,1)S(1)}, u32[]{:S(2)}, u32[]{:S(2)}) collective-permute-start(bf16[2,2,768]{2,1,0:T(2,128)(2,1)S(1)} %get-tuple-element.19), channel_id=1, source_target_pairs={{0,4},{4,8},{8,12},{12,16},{16,20},{20,24},{24,28},{1,5},{5,9},{9,... | collective-permute-start | bytes 18440 | tf_op jit(solution)/shard_map/ppermute | solution.py:16
  47.7 1.5 collective-permute-start.1
  49.2 0.3 fusion.37
  49.5 0.3 fusion.45
  49.8 0.1 bitcast_dynamic-update-slice_fusion
  49.9 2.1 %collective-permute-done.1 = bf16[2,2,768]{2,1,0:T(2,128)(2,1)S(1)} collective-permute-done((bf16[2,2,768]{2,1,0:T(2,128)(2,1)S(1)}, bf16[2,2,768]{2,1,0:T(2,128)(2,1)S(1)}, u32[]{:S(2)}, u32[]{:S(2)}) %collective-permute-start.1) | collective-permute-done | bytes 6176 | tf_op jit(solution)/shard_map/ppermute | solution.py:19
  52.0 0.3 fusion.34
  52.3 0.3 fusion.43
  52.6 2.5 %copy-done.5 = bf16[2,384,5,768]{3,1,2,0:T(8,128)(2,1)} copy-done((bf16[2,384,5,768]{3,1,2,0:T(8,128)(2,1)}, bf16[2,384,5,768]{3,1,2,0:T(8,128)(2,1)S(1)}, u32[]{:S(2)}) %copy-start.5) | copy-done | bytes 5898264
  55.1 7.7 %convolution_bitcast_fusion = f32[768,5,768]{2,0,1:T(8,128)} fusion(bf16[2,384,5,768]{3,1,2,0:T(8,128)(2,1)S(1)} %fusion.43, bf16[2,384,768]{2,1,0:T(8,128)(2,1)S(1)} %convert_element_type.39), kind=kOutput, calls=%fused_computation.14 | convolution fusion | flops 4529848320 | bytes 18874368 | tf_op jit(solution)/shard_map/blo,blki->oki/dot_general | solution.py:71
  62.9 0.0 reduce-scatter.7.cloned.1.call-start
  62.9 92.4 %reduce-scatter.5.cloned.1.call-done = f32[96,5,768]{2,0,1:T(8,128)} async-done(((f32[768,5,768]{2,0,1:T(8,128)}), f32[96,5,768]{2,0,1:T(8,128)}) %reduce-scatter.5.cloned.1.call-update) | async-done | bytes 1474576 | tf_op jit(solution)/shard_map/reduce_scatter | solution.py:70
  155.3 2.3 %copy.42 = f32[96,5,768]{0,1,2:T(8,128)S(1)} copy(f32[96,5,768]{2,0,1:T(8,128)} %reduce-scatter.5.cloned.1.call-done) | data formatting | bytes 2949120
  157.6 1.6 reshape.54
  159.2 10.8 %convert_add_fusion = f32[2,384,768]{2,1,0:T(8,128)} fusion(bf16[2,384,768]{2,1,0:T(8,128)(2,1)} %param.3, bf16[2,384,5,768]{3,1,2,0:T(8,128)(2,1)} %copy-done.5, bf16[5,768,768]{2,1,0:T(8,128)(2,1)} %param.4), kind=kOutput, calls=%fused_computation.6 | convolution fusion | flops 4531027968 | bytes 15335424 | tf_op jit(solution)/shard_map/blki,kio->blo/dot_general | solution.py:56
  170.0 3.0 %reshape.46 = f32[2,192,2,768]{3,2,1,0:T(2,128)S(1)} reshape(f32[2,384,768]{2,1,0:T(8,128)} %convert_add_fusion) | data formatting | bytes 4718592 | tf_op jit(solution)/shard_map/reshape | solution.py:58
  173.0 1.8 fusion.51
  174.9 0.2 fusion.49
  175.0 0.6 copy.32
  175.7 15.1 %all_to_all.18 = bf16[2,192,768]{1,0,2:T(2,128)(2,1)S(1)} all-to-all(bf16[2,192,768]{1,0,2:T(2,128)(2,1)S(1)} %copy.32), channel_id=1, replica_groups=mesh['seq'=8,'dp'=4] {'seq'}, dimensions={2} | all-to-all | bytes 1179648 | tf_op jit(solution)/shard_map/all_to_all | solution.py:60
  190.8 0.4 copy.33
  191.2 1.5 all_to_all.16
  192.7 1.9 reduce-scatter.7.cloned.1.call-done
  194.7 1.2 reshape.55
  195.9 0.9 copy.36
  (19 shorter events, 0.1 us)
Async XLA Ops:
  7.2 148.2 %reduce-scatter.5.cloned.1.call-start = ((), (), s32[]{:S(2)}) async-start(), calls=%async_computation.3 | async-start | bytes 13271040 | tf_op jit(solution)/shard_map/reduce_scatter | solution.py:70
  14.6 4.4 %copy-start.1 = (bf16[2,384,768]{2,1,0:T(8,128)(2,1)S(1)}, bf16[2,384,768]{2,1,0:T(8,128)(2,1)}, u32[]{:S(2)}) copy-start(bf16[2,384,768]{2,1,0:T(8,128)(2,1)} %param.3) | copy-start | bytes 3538948
  14.6 5.3 %copy-start.4 = (bf16[2,192,768]{2,1,0:T(8,128)(2,1)S(1)}, bf16[2,192,768]{2,1,0:T(8,128)(2,1)}, u32[]{:S(2)}) copy-start(bf16[2,192,768]{2,1,0:T(8,128)(2,1)} %get-tuple-element.20) | copy-start | bytes 1769476
  15.3 15.5 %collective-permute-start.2 = (bf16[2,2,768]{2,1,0:T(2,128)(2,1)}, bf16[2,2,768]{2,1,0:T(2,128)(2,1)S(1)}, u32[]{:S(2)}, u32[]{:S(2)}) collective-permute-start(bf16[2,2,768]{2,1,0:T(2,128)(2,1)} %get-tuple-element.17), channel_id=1, source_target_pairs={{0,4},{4,8},{8,12},{12,16},{16,20},{20,24},{24,28},{1,5},{5,9},{9,... | collective-permute-start | bytes 18440 | tf_op jit(solution)/shard_map/ppermute | solution.py:16
  17.7 14.6 %collective-permute-start.3 = (bf16[2,2,768]{2,1,0:T(2,128)(2,1)}, bf16[2,2,768]{2,1,0:T(2,128)(2,1)S(1)}, u32[]{:S(2)}, u32[]{:S(2)}) collective-permute-start(bf16[2,2,768]{2,1,0:T(2,128)(2,1)} %get-tuple-element.16), channel_id=1, source_target_pairs={{4,0},{8,4},{12,8},{16,12},{20,16},{24,20},{28,24},{5,1},{9,5},{13... | collective-permute-start | bytes 18440 | tf_op jit(solution)/shard_map/ppermute | solution.py:19
  30.9 1.3 copy-start.3
  32.1 2.7 %copy-start = (bf16[5,768,768]{2,1,0:T(8,128)(2,1)S(1)}, bf16[5,768,768]{2,1,0:T(8,128)(2,1)}, u32[]{:S(2)}) copy-start(bf16[5,768,768]{2,1,0:T(8,128)(2,1)} %rev.3) | copy-start | bytes 17694724
  32.2 2.9 %copy-start.2 = (bf16[2,384,768]{2,1,0:T(8,128)(2,1)S(1)}, bf16[2,384,768]{2,1,0:T(8,128)(2,1)}, u32[]{:S(2)}) copy-start(bf16[2,384,768]{2,1,0:T(8,128)(2,1)} %param.3) | copy-start | bytes 3538948
  32.2 2.9 %copy-start.7 = (f32[2,384]{1,0:T(2,128)S(1)}, f32[2,384]{1,0:T(2,128)}, u32[]{:S(2)}) copy-start(f32[2,384]{1,0:T(2,128)} %get-tuple-element.23) | copy-start | bytes 9220
  35.1 5.4 %copy-start.6 = (f32[2,384]{1,0:T(2,128)S(1)}, f32[2,384]{1,0:T(2,128)}, u32[]{:S(2)}) copy-start(f32[2,384]{1,0:T(2,128)} %get-tuple-element.22) | copy-start | bytes 9220
  42.6 6.6 %collective-permute-start = (bf16[2,2,768]{2,1,0:T(2,128)(2,1)S(1)}, bf16[2,2,768]{2,1,0:T(2,128)(2,1)S(1)}, u32[]{:S(2)}, u32[]{:S(2)}) collective-permute-start(bf16[2,2,768]{2,1,0:T(2,128)(2,1)S(1)} %get-tuple-element.19), channel_id=1, source_target_pairs={{0,4},{4,8},{8,12},{12,16},{16,20},{20,24},{24,28},{1,5},{5,9},{9,... | collective-permute-start | bytes 18440 | tf_op jit(solution)/shard_map/ppermute | solution.py:16
  47.7 4.3 %collective-permute-start.1 = (bf16[2,2,768]{2,1,0:T(2,128)(2,1)S(1)}, bf16[2,2,768]{2,1,0:T(2,128)(2,1)S(1)}, u32[]{:S(2)}, u32[]{:S(2)}) collective-permute-start(bf16[2,2,768]{2,1,0:T(2,128)(2,1)S(1)} %get-tuple-element.18), channel_id=1, source_target_pairs={{4,0},{8,4},{12,8},{16,12},{20,16},{24,20},{28,24},{5,1},{9,5},{13... | collective-permute-start | bytes 18440 | tf_op jit(solution)/shard_map/ppermute | solution.py:19
  52.6 2.5 %copy-start.5 = (bf16[2,384,5,768]{3,1,2,0:T(8,128)(2,1)}, bf16[2,384,5,768]{3,1,2,0:T(8,128)(2,1)S(1)}, u32[]{:S(2)}) copy-start(bf16[2,384,5,768]{3,1,2,0:T(8,128)(2,1)S(1)} %fusion.43) | copy-start | bytes 17694724
  62.9 131.8 %reduce-scatter.7.cloned.1.call-start = ((), (), s32[]{:S(2)}) async-start(), calls=%async_computation.4 | async-start | bytes 1966080
Sparse Core Ops, SparseCore 0:
  63.0 92.2 reduce-scatter.4
  159.4 35.2 reduce-scatter.6
where the time goes:
time: 204 us
  waiting for transfers between devices  96.5 us (47%)
  local copies, waits for them, and re-layouts  35.9 us (18%)
  matrix products  24 us (12%)
  blocking collectives  15.1 us (7%)
  between operations  14.3 us (7%)
  starting transfers between devices  10.3 us (5%)
  other arithmetic  7.48 us (4%)
    reduce_scatter x1, waiting for transfers between devices, shards(): lax.psum_scatter(jnp.einsum('blo,blki->oki', branch_grad, window, preferr...  92.4 us
    all_to_all x1, blocking collectives, shards(): lax.all_to_all(pooled, 'seq', split_axis=2, concat_axis=1, tiled=True)  15.1 us
    unnamed x22, local copies, waits for them, and re-layouts  11.6 us
    dot_general x1, matrix products, shards(): jnp.einsum('blki,kio->blo', window, weight, preferred_element_type=jnp.fl...  10.8 us
    dot_general x1, matrix products, shards(): jnp.einsum('blo,blki->oki', branch_grad, window, preferred_element_type=j...  7.74 us
    ppermute x2, starting transfers between devices, with_halo(): lax.ppermute(lax.slice_in_dim(block, block.shape[dim] - width, None, axis...  7.48 us
    rev x1, local copies, waits for them, and re-layouts, shards(): weight[::-1]  5.59 us
    dot_general x1, matrix products, shards(): jnp.einsum('blko,kio->bli', grad_window, weight[::-1], preferred_element_...  5.43 us
  transfers between devices with their start and end apart: 6, of which 3 were waited for; matrix products, arithmetic and copies ran while one was open for 15% of the time, Pallas kernels for 0%

commit v1 on v0

v1 whole, which is shorter than its diff:
```python
import functools

import jax
import jax.numpy as jnp
from jax import lax
from jax.experimental import pallas as pl
from jax.experimental.pallas import tpu as pltpu
from jax.sharding import PartitionSpec as P

epsilon = 1e-06
root_half = 0.7071067811865476
inv_root_two_pi = 0.3989422804014327
edge = 16
f32 = jnp.float32
bf16 = jnp.bfloat16


def phases(rows):
    inverse = lax.rsqrt(jnp.mean(rows * rows, axis=-1, keepdims=True) + epsilon)
    normed = rows * inverse
    cdf = 0.5 * (1.0 + lax.erf(normed * root_half))
    slope = cdf + normed * inv_root_two_pi * jnp.exp(-0.5 * normed * normed)
    return normed * cdf, slope * inverse


def kernel(
    n, zs, f_ref, w_ref, g_ref,
    trunk_ref, igrad_ref, wg_ref,
    halo_f, halo_g, acts, acts_sib, gext, gt, gt_sib, tslope, prod, part, recv, own,
    zpart, zrecv, zown, pooled, tpart,
    halo_send, halo_recv, sib_send, sib_recv, x_send, x_recv, z_send, z_recv, t_send, t_recv,
):
    batch, half, wide = f_ref.shape
    chans = wide // 2
    taps = w_ref.shape[0]
    rows = batch * half
    chips = n // 2
    oblk = chans // n
    iblk = chans // zs
    me = lax.axis_index("seq")
    core = lax.rem(me, 2)
    chip = me // 2
    sib = me + 1 - 2 * core
    zme = lax.axis_index("dp")

    barrier = pltpu.get_barrier_semaphore()
    for d in range(1, n):
        pl.semaphore_signal(barrier, inc=1, device_id={"seq": lax.rem(me + d, n)},
                            device_id_type=pl.DeviceIdType.MESH)
    for d in range(1, zs):
        pl.semaphore_signal(barrier, inc=1, device_id={"dp": lax.rem(zme + d, zs)},
                            device_id_type=pl.DeviceIdType.MESH)
    pl.semaphore_wait(barrier, n - 1 + zs - 1)

    def remote(src, dst, ssem, rsem, where):
        return pltpu.make_async_remote_copy(
            src_ref=src, dst_ref=dst, send_sem=ssem, recv_sem=rsem,
            device_id=where, device_id_type=pl.DeviceIdType.MESH)

    right = {"seq": lax.rem(me + 1, n)}
    left = {"seq": lax.rem(me + n - 1, n)}
    halos = []
    for side, (where, start) in enumerate(((right, half - edge), (left, 0))):
        halos.append(remote(f_ref.at[:, pl.ds(start, edge)], halo_f.at[side],
                            halo_send.at[2 * side], halo_recv.at[2 * side], where))
        halos.append(remote(g_ref.at[:, pl.ds(start, edge)], halo_g.at[side],
                            halo_send.at[2 * side + 1], halo_recv.at[2 * side + 1], where))
    for copy in halos:
        copy.start()

    chunk = 32
    per = half // chunk

    @pl.loop(0, batch * per)
    def _(step):
        b = step // per
        r = pl.multiple_of(lax.rem(step, per) * chunk, chunk)
        for p in range(2):
            block = f_ref[b, pl.ds(r, chunk), p * chans : (p + 1) * chans].astype(f32)
            act, slope = phases(block)
            acts[p, pl.ds(pl.multiple_of(b * half + r, chunk), chunk), :] = act.astype(bf16)
            tslope[b, pl.ds(r, chunk), p * chans : (p + 1) * chans] = slope

    to_sib = {"seq": sib}
    send_acts = remote(acts.at[:, pl.ds(0, rows)], acts_sib, sib_send.at[0], sib_recv.at[0], to_sib)
    send_acts.start()

    for copy in halos:
        copy.wait()
    index = lax.broadcasted_iota(jnp.int32, (edge, 1), 0)
    has_left = jnp.where(me > 0, 1.0, 0.0)
    has_right = jnp.where(me < n - 1, 1.0, 0.0)

    def edge_rows(ref, lanes):
        out = jnp.zeros((edge, lanes), f32)
        for b in range(batch):
            low = ref[0, b].astype(f32)[edge - 1 : edge, :] * has_left
            high = ref[1, b].astype(f32)[0:1, :] * has_right
            out = jnp.where(index == b, low, out)
            out = jnp.where(index == batch + b, high, out)
        return out

    hf = edge_rows(halo_f, wide)
    hg = 0.5 * edge_rows(halo_g, chans)
    for p in range(2):
        act, _ = phases(hf[:, p * chans : (p + 1) * chans])
        acts[p, pl.ds(rows, edge), :] = act.astype(bf16)
    gext[pl.ds(rows, edge), :] = hg.astype(bf16)

    spot = lax.broadcasted_iota(jnp.int32, (half, 1), 0)

    def later(block, b, tail):
        return jnp.where(spot == 0, tail[b : b + 1, :], pltpu.roll(block, 1, 0))

    def sooner(block, b, tail):
        return jnp.where(spot == half - 1, tail[batch + b : batch + b + 1, :],
                         pltpu.roll(block, half - 1, 0))

    for b in range(batch):
        g0 = 0.5 * g_ref[b].astype(f32)
        gext[pl.ds(b * half, half), :] = g0.astype(bf16)
        for s, shifted in enumerate((sooner(g0, b, hg), g0, later(g0, b, hg))):
            turned = shifted.T.astype(bf16)
            for o in range(n):
                gt[o % 2, s, b, o // 2] = turned[o * oblk : (o + 1) * oblk, :]
    send_gt = remote(gt.at[1 - core], gt_sib, sib_send.at[1], sib_recv.at[1], to_sib)
    send_gt.start()
    send_acts.wait_recv()
    send_gt.wait_recv()

    def product(s, p, slot):
        for m in range(chips):
            total = jnp.zeros((oblk, chans), f32)
            for b in range(batch):
                total += jnp.dot(gt[core, s, b, m], acts[p, b * half : (b + 1) * half, :],
                                 preferred_element_type=f32)
                total += jnp.dot(gt_sib[s, b, m], acts_sib[p, b * half : (b + 1) * half, :],
                                 preferred_element_type=f32)
            prod[slot, m] = total

    def x_copy(t, d):
        other = lax.rem(chip + d, chips)
        return remote(part.at[t, other], recv.at[t, d - 1], x_send.at[t, d - 1],
                      x_recv.at[t, d - 1], {"seq": 2 * other + core})

    product(0, 0, 0)

    @pl.loop(0, taps)
    def _(t):
        now = lax.rem(t + 1, 2)
        product((t + 1) // 2, lax.rem(t + 1, 2), now)
        for m in range(chips):
            part[t, m] = (prod[0, m] + prod[1, m]).astype(bf16)
        own[t] = prod[0, chip] + prod[1, chip]
        for d in range(1, chips):
            x_copy(t, d).start()

    cols = 256

    @pl.loop(0, chans // cols)
    def _(tile):
        c0 = pl.multiple_of(tile * cols, cols)
        w = [w_ref[k, :, pl.ds(c0, cols)] for k in range(taps)]

        def dots(pairs):
            return sum(jnp.dot(acts[p], w[k], preferred_element_type=f32) for p, k in pairs)

        before = dots(((0, 0), (1, 0), (1, 1)))
        middle = dots(((0, 1), (0, 2), (1, 2), (1, 3)))
        after = dots(((0, 3), (0, 4), (1, 4)))
        for b in range(batch):
            at = slice(b * half, (b + 1) * half)
            total = middle[at] + later(before[at], b, before[rows:]) + sooner(after[at], b, after[rows:])
            total += f_ref[b, :, pl.ds(c0, cols)].astype(f32)
            total += f_ref[b, :, pl.ds(chans + c0, cols)].astype(f32)
            pooled[b, :, pl.ds(c0, cols)] = 0.5 * total

    for b in range(batch):
        whole = pooled[b]
        for o in range(n):
            tpart[o, b] = whole[:, o * oblk : (o + 1) * oblk].astype(bf16)

    def t_copy(d):
        other = lax.rem(me + d, n)
        return remote(tpart.at[other], trunk_ref.at[:, pl.ds(pl.multiple_of(me * half, edge), half)],
                      t_send.at[d - 1], t_recv.at[d - 1], {"seq": other})

    for d in range(1, n):
        t_copy(d).start()
    trunk_ref[:, pl.ds(pl.multiple_of(me * half, edge), half), :] = tpart[me]

    def z_copy(t, d):
        other = lax.rem(zme + d, zs)
        return remote(zpart.at[t, other], zrecv.at[t, d - 1], z_send.at[t, d - 1],
                      z_recv.at[t, d - 1], {"dp": other})

    def collect(t):
        total = own[t]
        for d in range(1, chips):
            x_copy(t, d).wait_recv()
        for d in range(1, chips):
            total += recv[t, d - 1].astype(f32)
        for q in range(zs):
            piece = total[:, q * iblk : (q + 1) * iblk]
            zown[t, q] = piece
            zpart[t, q] = piece.astype(bf16)
        for d in range(1, zs):
            z_copy(t, d).start()

    @pl.loop(0, 2)
    def _(t):
        collect(t)

    @pl.loop(0, chans // cols)
    def _(tile):
        c0 = pl.multiple_of(tile * cols, cols)
        q = [
            lax.dot_general(gext[...], w_ref[k, pl.ds(c0, cols), :], (((1,), (1,)), ((), ())),
                            preferred_element_type=f32)
            for k in range(taps)
        ]
        q01, q12, q23, q34 = q[0] + q[1], q[1] + q[2], q[2] + q[3], q[3] + q[4]
        for b in range(batch):
            at = slice(b * half, (b + 1) * half)
            even = q12[at] + sooner(q[0][at], b, q[0][rows:]) + later(q34[at], b, q34[rows:])
            odd = q23[at] + sooner(q01[at], b, q01[rows:]) + later(q[4][at], b, q[4][rows:])
            tslope[b, :, pl.ds(c0, cols)] = tslope[b, :, pl.ds(c0, cols)] * even
            tslope[b, :, pl.ds(chans + c0, cols)] = tslope[b, :, pl.ds(chans + c0, cols)] * odd

    @pl.loop(0, batch * per)
    def _(step):
        b = step // per
        r = pl.multiple_of(lax.rem(step, per) * chunk, chunk)
        up = 0.5 * g_ref[b, pl.ds(r, chunk), :].astype(f32)
        for p in range(2):
            lanes = slice(p * chans, (p + 1) * chans)
            block = f_ref[b, pl.ds(r, chunk), lanes].astype(f32)
            scaled = tslope[b, pl.ds(r, chunk), lanes]
            inverse = lax.rsqrt(jnp.mean(block * block, axis=-1, keepdims=True) + epsilon)
            centred = jnp.mean(scaled * block, axis=-1, keepdims=True) * inverse * inverse
            igrad_ref[b, pl.ds(r, chunk), lanes] = (up + scaled - block * centred).astype(bf16)

    @pl.loop(2, taps)
    def _(t):
        collect(t)

    @pl.loop(0, taps)
    def _(t):
        total = zown[t, zme]
        for d in range(1, zs):
            z_copy(t, d).wait_recv()
        for d in range(1, zs):
            total += zrecv[t, d - 1].astype(f32)
        wg_ref[t] = total
        for d in range(1, zs):
            z_copy(t, d).wait_send()
        for d in range(1, chips):
            x_copy(t, d).wait_send()

    for d in range(1, n):
        t_copy(d).wait()
    send_acts.wait_send()
    send_gt.wait_send()


def shards(features, weight, cotangent):
    n = lax.axis_size("seq")
    zs = lax.axis_size("dp")
    taps, _, chans = weight.shape
    batch, length, _ = features.shape
    half = length // 2
    rows = batch * half
    chips = n // 2
    oblk = chans // n
    iblk = chans // zs
    paired = features.reshape(batch, half, 2 * chans)
    vmem = pl.BlockSpec(memory_space=pltpu.VMEM)
    dma = pltpu.SemaphoreType.DMA
    trunk, igrad, wg = pl.pallas_call(
        functools.partial(kernel, n, zs),
        out_shape=(
            jax.ShapeDtypeStruct((batch, half * n, oblk), bf16),
            jax.ShapeDtypeStruct((batch, half, 2 * chans), bf16),
            jax.ShapeDtypeStruct((taps, oblk, iblk), f32),
        ),
        in_specs=[vmem] * 3,
        out_specs=(vmem,) * 3,
        scratch_shapes=[
            pltpu.VMEM((2, batch, edge, 2 * chans), bf16),
            pltpu.VMEM((2, batch, edge, chans), bf16),
            pltpu.VMEM((2, rows + edge, chans), bf16),
            pltpu.VMEM((2, rows, chans), bf16),
            pltpu.VMEM((rows + edge, chans), bf16),
            pltpu.VMEM((2, 3, batch, chips, oblk, half), bf16),
            pltpu.VMEM((3, batch, chips, oblk, half), bf16),
            pltpu.VMEM((batch, half, 2 * chans), f32),
            pltpu.VMEM((2, chips, oblk, chans), f32),
            pltpu.VMEM((taps, chips, oblk, chans), bf16),
            pltpu.VMEM((taps, chips - 1, oblk, chans), bf16),
            pltpu.VMEM((taps, oblk, chans), f32),
            pltpu.VMEM((taps, zs, oblk, iblk), bf16),
            pltpu.VMEM((taps, zs - 1, oblk, iblk), bf16),
            pltpu.VMEM((taps, zs, oblk, iblk), f32),
            pltpu.VMEM((batch, half, chans), f32),
            pltpu.VMEM((n, batch, half, oblk), bf16),
            dma((4,)), dma((4,)), dma((2,)), dma((2,)),
            dma((taps, chips - 1)), dma((taps, chips - 1)),
            dma((taps, zs - 1)), dma((taps, zs - 1)),
            dma((n - 1,)), dma((n - 1,)),
        ],
        compiler_params=pltpu.CompilerParams(
            collective_id=0, has_side_effects=True, vmem_limit_bytes=60 * 1024 * 1024
        ),
        cost_estimate=pl.CostEstimate(
            flops=2 * rows * chans * chans * 21, bytes_accessed=12_000_000, transcendentals=4 * rows * chans
        ),
    )(paired, weight, cotangent)
    return trunk, igrad.reshape(batch, length, chans), jnp.swapaxes(wg, 1, 2)


def solution(mesh):
    return jax.shard_map(
        shards,
        mesh=mesh,
        in_specs=(P("dp", "seq", None), P(), P("dp", "seq", None)),
        out_specs=(P("dp", None, "seq"), P("dp", "seq", None), P(None, "dp", "seq")),
        check_vma=False,
    )
```

time: 204 us -> 70.2 us (0.34)
  waiting for transfers between devices: 96.5 us -> 0 us
  Pallas kernels: 0 us -> 61.8 us
  local copies, waits for them, and re-layouts: 35.9 us -> 7.5 us
  matrix products: 24 us -> 0 us
  blocking collectives: 15.1 us -> 0 us
  between operations: 14.3 us -> 0.66 us
  starting transfers between devices: 10.3 us -> 0 us
  other arithmetic: 7.48 us -> 0 us
    reduce_scatter x1 -> x0, waiting for transfers between devices: 92.4 us -> none  [shards(): lax.psum_scatter(jnp.einsum('blo,blki->oki', branch_grad, window, preferr...]
    pallas_call x0 -> x1, Pallas kernels: none -> 61.8 us  [shards(): pl.pallas_call(functools.partial(kernel, n, zs), out_shape=(jax.ShapeDtyp...]
    dot_general x3 -> x0, matrix products: 24 us -> none  [the longest x1 10.8 us: shards(): jnp.einsum('blki,kio->blo', window, weight, preferred_element_type=jnp.fl...]
    all_to_all x1 -> x0, blocking collectives: 15.1 us -> none  [shards(): lax.all_to_all(pooled, 'seq', split_axis=2, concat_axis=1, tiled=True)]
    ppermute x4 -> x0, starting transfers between devices: 10.2 us -> none  [the longest x2 7.48 us: with_halo(): lax.ppermute(lax.slice_in_dim(block, block.shape[dim] - width, None, axis...]
    unnamed x22 -> x6, local copies, waits for them, and re-layouts: 11.6 us -> 3.34 us
    rev x1 -> x0, local copies, waits for them, and re-layouts: 5.59 us -> none  [shards(): weight[::-1]]
    convert_element_type x2 -> x0, local copies, waits for them, and re-layouts: 4.38 us -> none  [the longest x1 3.74 us: shards(): branch_grad = upward.astype(jnp.bfloat16)]
  transfers between devices with their start and end apart: 6 -> 0, of which waited for: 3 -> 0; matrix products, arithmetic and copies ran while one was open for 15% -> 0% of each run, Pallas kernels for 0% -> 0%
where the time goes in v1:
time: 70.2 us; the launch traced here: 70 us
  Pallas kernels  61.8 us (88%)
  local copies, waits for them, and re-layouts  7.5 us (11%)
    pallas_call x1, Pallas kernels, shards(): pl.pallas_call(functools.partial(kernel, n, zs), out_shape=(jax.ShapeDtyp...  61.8 us
    unnamed x6, local copies, waits for them, and re-layouts  3.34 us
    reshape x1, local copies, waits for them, and re-layouts, shards(): paired = features.reshape(batch, half, 2 * chans)  2.95 us

profile of v1, /device:TPU:0, one launch (start us, length us, event | category | flops | bytes accessed | tf_op | source)
XLA Modules:
  0.0 70.0 jit_solution(16759114194651867115)
XLA Ops:
  0.6 2.9 %reshape.12.f_ref = bf16[2,192,1536]{2,1,0:T(8,128)(2,1)} reshape(bf16[2,384,768]{2,1,0:T(8,128)(2,1)} %param.3) | data formatting | bytes 2359296 | tf_op jit(solution)/shard_map/reshape | solution.py:276
  3.6 61.8 %shard_map.58 = (bf16[2,1536,96]{2,1,0:T(8,128)(2,1)}, bf16[2,192,1536]{2,1,0:T(8,128)(2,1)}, f32[5,96,192]{2,1,0:T(8,128)}) custom-call(bf16[2,192,1536]{2,1,0:T(8,128)(2,1)} %reshape.12.f_ref, bf16[5,768,768]{2,1,0:T(8,128)(2,1)} %w_ref.1, bf16[2,192,768]{2,1,0:T(8,128)(2,1)} %g_ref.1), custom_call_target="tpu_custom_call" | custom-call | flops 9512681472 | bytes 12000000 | tf_op jit(solution)/shard_map/pallas_call | solution.py:279
  65.4 0.0 copy-start.1
  65.4 0.0 copy-start
  65.5 2.3 %copy.6 = bf16[2,1536,96]{1,2,0:T(8,128)(2,1)} copy(bf16[2,1536,96]{2,1,0:T(8,128)(2,1)} %get-tuple-element.9) | data formatting | bytes 1179648
  67.8 0.0 copy-done.1
  67.8 1.0 %copy.7 = f32[5,192,96]{2,1,0:T(8,128)} copy(f32[5,192,96]{1,2,0:T(8,128)S(1)} %bitcast.1) | data formatting | bytes 737280
  68.8 0.0 copy-done
  68.8 1.2 %reshape.13 = bf16[2,384,768]{2,1,0:T(8,128)(2,1)} reshape(bf16[2,192,1536]{2,1,0:T(8,128)(2,1)S(1)} %copy-done) | data formatting | bytes 2359296 | tf_op jit(solution)/shard_map/reshape | solution.py:318
Async XLA Ops:
  65.4 2.4 %copy-start.1 = (f32[5,96,192]{2,1,0:T(8,128)S(1)}, f32[5,96,192]{2,1,0:T(8,128)}, u32[]{:S(2)}) copy-start(f32[5,96,192]{2,1,0:T(8,128)} %get-tuple-element.8) | copy-start | bytes 1105924
  65.4 3.4 %copy-start = (bf16[2,192,1536]{2,1,0:T(8,128)(2,1)S(1)}, bf16[2,192,1536]{2,1,0:T(8,128)(2,1)}, u32[]{:S(2)}) copy-start(bf16[2,192,1536]{2,1,0:T(8,128)(2,1)} %get-tuple-element.7) | copy-start | bytes 3538948

commit v2 on v1

--- a/solution.py
+++ b/solution.py
@@ -24,15 +24,15 @@
 
 
 def kernel(
-    n, zs, f_ref, w_ref, g_ref,
+    n, zs, f_ref, w_hbm, g_ref,
     trunk_ref, igrad_ref, wg_ref,
-    halo_f, halo_g, acts, acts_sib, gext, gt, gt_sib, tslope, prod, part, recv, own,
+    w_ref, fd, stage, halo_f, halo_g, acts, acts_sib, gext, gt, gt_sib, tslope, prod, part, recv, part2, recv2, keep, own,
     zpart, zrecv, zown, pooled, tpart,
-    halo_send, halo_recv, sib_send, sib_recv, x_send, x_recv, z_send, z_recv, t_send, t_recv,
+    w_sem, halo_send, halo_recv, sib_send, sib_recv, x_send, x_recv, y_send, y_recv, z_send, z_recv, t_send, t_recv,
 ):
-    batch, half, wide = f_ref.shape
-    chans = wide // 2
-    taps = w_ref.shape[0]
+    batch, length, chans = f_ref.shape
+    half = length // 2
+    taps = w_hbm.shape[0]
     rows = batch * half
     chips = n // 2
     oblk = chans // n
@@ -43,6 +43,8 @@
     sib = me + 1 - 2 * core
     zme = lax.axis_index("dp")
 
+    load = pltpu.make_async_copy(w_hbm, w_ref, w_sem.at[0])
+    load.start()
     barrier = pltpu.get_barrier_semaphore()
     for d in range(1, n):
         pl.semaphore_signal(barrier, inc=1, device_id={"seq": lax.rem(me + d, n)},
@@ -60,8 +62,10 @@
     right = {"seq": lax.rem(me + 1, n)}
     left = {"seq": lax.rem(me + n - 1, n)}
     halos = []
-    for side, (where, start) in enumerate(((right, half - edge), (left, 0))):
-        halos.append(remote(f_ref.at[:, pl.ds(start, edge)], halo_f.at[side],
+    for side, (where, start_last) in enumerate(((right, True), (left, False))):
+        start = half - edge if start_last else 0
+        f_start = length - edge if start_last else 0
+        halos.append(remote(f_ref.at[:, pl.ds(f_start, edge)], halo_f.at[side],
                             halo_send.at[2 * side], halo_recv.at[2 * side], where))
         halos.append(remote(g_ref.at[:, pl.ds(start, edge)], halo_g.at[side],
                             halo_send.at[2 * side + 1], halo_recv.at[2 * side + 1], where))
@@ -71,19 +75,30 @@
     chunk = 32
     per = half // chunk
 
-    @pl.loop(0, batch * per)
-    def _(step):
-        b = step // per
-        r = pl.multiple_of(lax.rem(step, per) * chunk, chunk)
-        for p in range(2):
-            block = f_ref[b, pl.ds(r, chunk), p * chans : (p + 1) * chans].astype(f32)
-            act, slope = phases(block)
-            acts[p, pl.ds(pl.multiple_of(b * half + r, chunk), chunk), :] = act.astype(bf16)
-            tslope[b, pl.ds(r, chunk), p * chans : (p + 1) * chans] = slope
+    def activate(b):
+        @pl.loop(0, per)
+        def _(step):
+            r = pl.multiple_of(step * chunk, chunk)
+            raw = f_ref[b, pl.ds(pl.multiple_of(2 * r, chunk), 2 * chunk), :].astype(f32)
+            for c in range(chans // 128):
+                stage[c] = raw[:, c * 128 : (c + 1) * 128]
+            for p in range(2):
+                block = jnp.concatenate(
+                    [stage[c, pl.ds(p, chunk, stride=2), :] for c in range(chans // 128)], axis=1)
+                act, slope = phases(block)
+                fd[b, pl.ds(r, chunk), p * chans : (p + 1) * chans] = block.astype(bf16)
+                acts[p, pl.ds(pl.multiple_of(b * half + r, chunk), chunk), :] = act.astype(bf16)
+                tslope[b, pl.ds(r, chunk), p * chans : (p + 1) * chans] = slope
 
     to_sib = {"seq": sib}
-    send_acts = remote(acts.at[:, pl.ds(0, rows)], acts_sib, sib_send.at[0], sib_recv.at[0], to_sib)
-    send_acts.start()
+
+    def sib_copy(b):
+        at = pl.ds(b * half, half)
+        return remote(acts.at[:, at], acts_sib.at[:, at], sib_send.at[b + 1], sib_recv.at[b + 1], to_sib)
+
+    for b in range(batch - 1):
+        activate(b)
+        sib_copy(b).start()
 
     for copy in halos:
         copy.wait()
@@ -91,20 +106,16 @@
     has_left = jnp.where(me > 0, 1.0, 0.0)
     has_right = jnp.where(me < n - 1, 1.0, 0.0)
 
-    def edge_rows(ref, lanes):
-        out = jnp.zeros((edge, lanes), f32)
+    def edge_rows(ref, last, first):
+        out = jnp.zeros((edge, chans), f32)
         for b in range(batch):
-            low = ref[0, b].astype(f32)[edge - 1 : edge, :] * has_left
-            high = ref[1, b].astype(f32)[0:1, :] * has_right
+            low = ref[0, b].astype(f32)[last : last + 1, :] * has_left
+            high = ref[1, b].astype(f32)[first : first + 1, :] * has_right
             out = jnp.where(index == b, low, out)
             out = jnp.where(index == batch + b, high, out)
         return out
 
-    hf = edge_rows(halo_f, wide)
-    hg = 0.5 * edge_rows(halo_g, chans)
-    for p in range(2):
-        act, _ = phases(hf[:, p * chans : (p + 1) * chans])
-        acts[p, pl.ds(rows, edge), :] = act.astype(bf16)
+    hg = 0.5 * edge_rows(halo_g, edge - 1, 0)
     gext[pl.ds(rows, edge), :] = hg.astype(bf16)
 
     spot = lax.broadcasted_iota(jnp.int32, (half, 1), 0)
@@ -123,10 +134,16 @@
             turned = shifted.T.astype(bf16)
             for o in range(n):
                 gt[o % 2, s, b, o // 2] = turned[o * oblk : (o + 1) * oblk, :]
-    send_gt = remote(gt.at[1 - core], gt_sib, sib_send.at[1], sib_recv.at[1], to_sib)
+    send_gt = remote(gt.at[1 - core], gt_sib, sib_send.at[0], sib_recv.at[0], to_sib)
     send_gt.start()
-    send_acts.wait_recv()
+    activate(batch - 1)
+    sib_copy(batch - 1).start()
+    for p in range(2):
+        act, _ = phases(edge_rows(halo_f, edge - 2 + p, p))
+        acts[p, pl.ds(rows, edge), :] = act.astype(bf16)
     send_gt.wait_recv()
+    for b in range(batch):
+        sib_copy(b).wait_recv()
 
     def product(s, p, slot):
         for m in range(chips):
@@ -138,27 +155,64 @@
                                  preferred_element_type=f32)
             prod[slot, m] = total
 
+    square = chips == 4
+    hblk = oblk // 2
+    x = lax.rem(chip, 2)
+    y = chip // 2
+    beside = chip + 1 - 2 * x
+    beyond = chip + 2 - 4 * y
+    across = beside + 2 - 4 * y
+    near = ((beside, slice(0, hblk)), (beyond, slice(hblk, oblk)))
+
     def x_copy(t, d):
-        other = lax.rem(chip + d, chips)
-        return remote(part.at[t, other], recv.at[t, d - 1], x_send.at[t, d - 1],
-                      x_recv.at[t, d - 1], {"seq": 2 * other + core})
+        if square:
+            return remote(part.at[t, d], recv.at[t, d], x_send.at[t, d], x_recv.at[t, d],
+                          {"seq": 2 * near[d][0] + core})
+        other = lax.rem(chip + d + 1, chips)
+        return remote(part.at[t, other], recv.at[t, d], x_send.at[t, d],
+                      x_recv.at[t, d], {"seq": 2 * other + core})
+
+    def y_copy(t, h):
+        return remote(part2.at[t, h], recv2.at[t, h], y_send.at[t, h], y_recv.at[t, h],
+                      {"seq": 2 * near[1 - h][0] + core})
+
+    firsts = 2 if square else chips - 1
+
+    def tap(t):
+        product((t + 1) // 2, lax.rem(t + 1, 2), lax.rem(t + 1, 2))
+
+        def both(m, at=slice(None)):
+            return prod[0, m, at] + prod[1, m, at]
+
+        if square:
+            for h in range(2):
+                at = near[h][1]
+                part[t, h, 0] = both(near[h][0], at).astype(bf16)
+                part[t, h, 1] = both(across, at).astype(bf16)
+                keep[t, h] = both(near[1 - h][0], at)
+        else:
+            for m in range(chips):
+                part[t, m] = both(m).astype(bf16)
+        for d in range(firsts):
+            x_copy(t, d).start()
+        own[t] = both(chip)
+
+    def forward(t):
+        if square:
+            for h in range(2):
+                x_copy(t, h).wait_recv()
+                part2[t, h] = (keep[t, h] + recv[t, h, 1].astype(f32)).astype(bf16)
+                y_copy(t, h).start()
 
     product(0, 0, 0)
-
-    @pl.loop(0, taps)
-    def _(t):
-        now = lax.rem(t + 1, 2)
-        product((t + 1) // 2, lax.rem(t + 1, 2), now)
-        for m in range(chips):
-            part[t, m] = (prod[0, m] + prod[1, m]).astype(bf16)
-        own[t] = prod[0, chip] + prod[1, chip]
-        for d in range(1, chips):
-            x_copy(t, d).start()
+    tap(0)
+    load.wait()
 
     cols = 256
 
     @pl.loop(0, chans // cols)
     def _(tile):
+        tap(tile + 1)
         c0 = pl.multiple_of(tile * cols, cols)
         w = [w_ref[k, :, pl.ds(c0, cols)] for k in range(taps)]
 
@@ -171,9 +225,14 @@
         for b in range(batch):
             at = slice(b * half, (b + 1) * half)
             total = middle[at] + later(before[at], b, before[rows:]) + sooner(after[at], b, after[rows:])
-            total += f_ref[b, :, pl.ds(c0, cols)].astype(f32)
-            total += f_ref[b, :, pl.ds(chans + c0, cols)].astype(f32)
+            total += fd[b, :, pl.ds(c0, cols)].astype(f32)
+            total += fd[b, :, pl.ds(chans + c0, cols)].astype(f32)
             pooled[b, :, pl.ds(c0, cols)] = 0.5 * total
+        forward(tile)
+
+    tiles = chans // cols
+    for t in range(tiles + 1, taps):
+        tap(t)
 
     for b in range(batch):
         whole = pooled[b]
@@ -195,21 +254,23 @@
                       z_recv.at[t, d - 1], {"dp": other})
 
     def collect(t):
-        total = own[t]
-        for d in range(1, chips):
-            x_copy(t, d).wait_recv()
-        for d in range(1, chips):
-            total += recv[t, d - 1].astype(f32)
+        if square:
+            for h in range(2):
+                y_copy(t, h).wait_recv()
+            total = own[t] + jnp.concatenate(
+                [recv[t, h, 0].astype(f32) + recv2[t, h].astype(f32) for h in range(2)], axis=0)
+        else:
+            total = own[t]
+            for d in range(firsts):
+                x_copy(t, d).wait_recv()
+            for d in range(firsts):
+                total += recv[t, d].astype(f32)
         for q in range(zs):
             piece = total[:, q * iblk : (q + 1) * iblk]
             zown[t, q] = piece
             zpart[t, q] = piece.astype(bf16)
         for d in range(1, zs):
             z_copy(t, d).start()
-
-    @pl.loop(0, 2)
-    def _(t):
-        collect(t)
 
     @pl.loop(0, chans // cols)
     def _(tile):
@@ -227,6 +288,12 @@
             tslope[b, :, pl.ds(c0, cols)] = tslope[b, :, pl.ds(c0, cols)] * even
             tslope[b, :, pl.ds(chans + c0, cols)] = tslope[b, :, pl.ds(chans + c0, cols)] * odd
 
+        @pl.when(tile < taps - tiles)
+        def _():
+            forward(tiles + tile)
+
+        collect(tile)
+
     @pl.loop(0, batch * per)
     def _(step):
         b = step // per
@@ -234,13 +301,17 @@
         up = 0.5 * g_ref[b, pl.ds(r, chunk), :].astype(f32)
         for p in range(2):
             lanes = slice(p * chans, (p + 1) * chans)
-            block = f_ref[b, pl.ds(r, chunk), lanes].astype(f32)
+            block = fd[b, pl.ds(r, chunk), lanes].astype(f32)
             scaled = tslope[b, pl.ds(r, chunk), lanes]
             inverse = lax.rsqrt(jnp.mean(block * block, axis=-1, keepdims=True) + epsilon)
             centred = jnp.mean(scaled * block, axis=-1, keepdims=True) * inverse * inverse
-            igrad_ref[b, pl.ds(r, chunk), lanes] = (up + scaled - block * centred).astype(bf16)
-
-    @pl.loop(2, taps)
+            result = up + scaled - block * centred
+            for c in range(chans // 128):
+                stage[c, pl.ds(p, chunk, stride=2), :] = result[:, c * 128 : (c + 1) * 128]
+        mixed = jnp.concatenate([stage[c] for c in range(chans // 128)], axis=1)
+        igrad_ref[b, pl.ds(pl.multiple_of(2 * r, chunk), 2 * chunk), :] = mixed.astype(bf16)
+
+    @pl.loop(tiles, taps)
     def _(t):
         collect(t)
 
@@ -254,12 +325,16 @@
         wg_ref[t] = total
         for d in range(1, zs):
             z_copy(t, d).wait_send()
-        for d in range(1, chips):
+        for d in range(firsts):
             x_copy(t, d).wait_send()
+        if square:
+            for h in range(2):
+                y_copy(t, h).wait_send()
 
     for d in range(1, n):
         t_copy(d).wait()
-    send_acts.wait_send()
+    for b in range(batch):
+        sib_copy(b).wait_send()
     send_gt.wait_send()
 
 
@@ -273,20 +348,28 @@
     chips = n // 2
     oblk = chans // n
     iblk = chans // zs
-    paired = features.reshape(batch, half, 2 * chans)
+    square = chips == 4
+    hblk = oblk // 2
+    firsts = 2 if square else chips - 1
+    sends = (taps, 2, 2, hblk, chans) if square else (taps, chips, oblk, chans)
+    lands = sends if square else (taps, chips - 1, oblk, chans)
+    relay = (taps, 2, hblk, chans) if square else (1, 1, 16, 128)
     vmem = pl.BlockSpec(memory_space=pltpu.VMEM)
     dma = pltpu.SemaphoreType.DMA
     trunk, igrad, wg = pl.pallas_call(
         functools.partial(kernel, n, zs),
         out_shape=(
             jax.ShapeDtypeStruct((batch, half * n, oblk), bf16),
-            jax.ShapeDtypeStruct((batch, half, 2 * chans), bf16),
+            jax.ShapeDtypeStruct((batch, length, chans), bf16),
             jax.ShapeDtypeStruct((taps, oblk, iblk), f32),
         ),
-        in_specs=[vmem] * 3,
+        in_specs=[vmem, pl.BlockSpec(memory_space=pl.ANY), vmem],
         out_specs=(vmem,) * 3,
         scratch_shapes=[
-            pltpu.VMEM((2, batch, edge, 2 * chans), bf16),
+            pltpu.VMEM(weight.shape, bf16),
+            pltpu.VMEM((batch, half, 2 * chans), bf16),
+            pltpu.VMEM((chans // 128, 64, 128), f32),
+            pltpu.VMEM((2, batch, edge, chans), bf16),
             pltpu.VMEM((2, batch, edge, chans), bf16),
             pltpu.VMEM((2, rows + edge, chans), bf16),
             pltpu.VMEM((2, rows, chans), bf16),
@@ -295,16 +378,19 @@
             pltpu.VMEM((3, batch, chips, oblk, half), bf16),
             pltpu.VMEM((batch, half, 2 * chans), f32),
             pltpu.VMEM((2, chips, oblk, chans), f32),
-            pltpu.VMEM((taps, chips, oblk, chans), bf16),
-            pltpu.VMEM((taps, chips - 1, oblk, chans), bf16),
+            pltpu.VMEM(sends, bf16),
+            pltpu.VMEM(lands, bf16),
+            pltpu.VMEM(relay, bf16),
+            pltpu.VMEM(relay, bf16),
+            pltpu.VMEM(relay, f32),
             pltpu.VMEM((taps, oblk, chans), f32),
             pltpu.VMEM((taps, zs, oblk, iblk), bf16),
             pltpu.VMEM((taps, zs - 1, oblk, iblk), bf16),
             pltpu.VMEM((taps, zs, oblk, iblk), f32),
             pltpu.VMEM((batch, half, chans), f32),
             pltpu.VMEM((n, batch, half, oblk), bf16),
-            dma((4,)), dma((4,)), dma((2,)), dma((2,)),
-            dma((taps, chips - 1)), dma((taps, chips - 1)),
+            dma((1,)), dma((4,)), dma((4,)), dma((batch + 1,)), dma((batch + 1,)),
+            dma((taps, firsts)), dma((taps, firsts)), dma((taps, 2)), dma((taps, 2)),
             dma((taps, zs - 1)), dma((taps, zs - 1)),
             dma((n - 1,)), dma((n - 1,)),
         ],
@@ -314,8 +400,8 @@
         cost_estimate=pl.CostEstimate(
             flops=2 * rows * chans * chans * 21, bytes_accessed=12_000_000, transcendentals=4 * rows * chans
         ),
-    )(paired, weight, cotangent)
-    return trunk, igrad.reshape(batch, length, chans), jnp.swapaxes(wg, 1, 2)
+    )(features, weight, cotangent)
+    return trunk, igrad, jnp.swapaxes(wg, 1, 2)
 
 
 def solution(mesh):

time: 70.2 us -> 66.2 us (0.943)
  local copies, waits for them, and re-layouts: 7.5 us -> 4.36 us
  Pallas kernels: 61.8 us -> 61 us
    reshape x2 -> x0, local copies, waits for them, and re-layouts: 4.16 us -> none  [the longest x1 2.95 us: shards(): paired = features.reshape(batch, half, 2 * chans)]
    unnamed x6 -> x7, local copies, waits for them, and re-layouts: 3.34 us -> 4.36 us
    pallas_call x1, Pallas kernels: 61.8 us -> 61 us  [shards(): pl.pallas_call(functools.partial(kernel, n, zs), out_shape=(jax.ShapeDtyp...]
where the time goes in v2:
time: 66.2 us; the launch traced here: 66 us
  Pallas kernels  61 us (92%)
  local copies, waits for them, and re-layouts  4.36 us (7%)
    pallas_call x1, Pallas kernels, shards(): pl.pallas_call(functools.partial(kernel, n, zs), out_shape=(jax.ShapeDtyp...  61 us
    unnamed x7, local copies, waits for them, and re-layouts  4.36 us

profile of v2, /device:TPU:0, one launch (start us, length us, event | category | flops | bytes accessed | tf_op | source)
XLA Modules:
  0.0 66.0 jit_solution(18105633680841624132)
XLA Ops:
  0.6 61.0 %shard_map.58 = (bf16[2,1536,96]{2,1,0:T(8,128)(2,1)}, bf16[2,384,768]{2,1,0:T(8,128)(2,1)}, f32[5,96,192]{2,1,0:T(8,128)}) custom-call(bf16[2,384,768]{2,1,0:T(8,128)(2,1)} %f_ref.1, bf16[5,768,768]{2,1,0:T(8,128)(2,1)} %w_hbm.1, bf16[2,192,768]{2,1,0:T(8,128)(2,1)} %g_ref.1), custom_call_target="tpu_custom_call" | custom-call | flops 9512681472 | bytes 12000000 | tf_op jit(solution)/shard_map/pallas_call | solution.py:359
  61.6 0.0 copy-start.1
  61.6 0.0 copy-start
  61.6 2.3 %copy.6 = bf16[2,1536,96]{1,2,0:T(8,128)(2,1)} copy(bf16[2,1536,96]{2,1,0:T(8,128)(2,1)} %get-tuple-element.9) | data formatting | bytes 1179648
  64.0 0.0 copy-done.1
  64.0 1.0 %copy.7 = f32[5,192,96]{2,1,0:T(8,128)} copy(f32[5,192,96]{1,2,0:T(8,128)S(1)} %bitcast.1) | data formatting | bytes 737280
  65.0 0.0 copy-done
  65.0 1.0 %copy.9 = bf16[2,384,768]{2,1,0:T(8,128)(2,1)} copy(bf16[2,384,768]{2,1,0:T(8,128)(2,1)S(1)} %copy-done) | data formatting | bytes 2359296
Async XLA Ops:
  61.6 2.4 %copy-start.1 = (f32[5,96,192]{2,1,0:T(8,128)S(1)}, f32[5,96,192]{2,1,0:T(8,128)}, u32[]{:S(2)}) copy-start(f32[5,96,192]{2,1,0:T(8,128)} %get-tuple-element.8) | copy-start | bytes 1105924
  61.6 3.4 %copy-start = (bf16[2,384,768]{2,1,0:T(8,128)(2,1)S(1)}, bf16[2,384,768]{2,1,0:T(8,128)(2,1)}, u32[]{:S(2)}) copy-start(bf16[2,384,768]{2,1,0:T(8,128)(2,1)} %get-tuple-element.16) | copy-start | bytes 3538948

commit v3 on v2

--- a/solution.py
+++ b/solution.py
@@ -26,8 +26,8 @@
 def kernel(
     n, zs, f_ref, w_hbm, g_ref,
     trunk_ref, igrad_ref, wg_ref,
-    w_ref, fd, stage, halo_f, halo_g, acts, acts_sib, gext, gt, gt_sib, tslope, prod, part, recv, part2, recv2, keep, own,
-    zpart, zrecv, zown, pooled, tpart,
+    w_ref, fd, stage, halo_f, halo_g, acts, gext, gt_all, gt_out, tslope, prod, part, recv, part2, recv2, keep, own,
+    zpart, zrecv, zown, pooled, tpart, tland,
     w_sem, halo_send, halo_recv, sib_send, sib_recv, x_send, x_recv, y_send, y_recv, z_send, z_recv, t_send, t_recv,
 ):
     batch, length, chans = f_ref.shape
@@ -87,14 +87,14 @@
                     [stage[c, pl.ds(p, chunk, stride=2), :] for c in range(chans // 128)], axis=1)
                 act, slope = phases(block)
                 fd[b, pl.ds(r, chunk), p * chans : (p + 1) * chans] = block.astype(bf16)
-                acts[p, pl.ds(pl.multiple_of(b * half + r, chunk), chunk), :] = act.astype(bf16)
+                acts[p, pl.ds(pl.multiple_of(edge + b * half + r, edge), chunk), :] = act.astype(bf16)
                 tslope[b, pl.ds(r, chunk), p * chans : (p + 1) * chans] = slope
 
     to_sib = {"seq": sib}
 
     def sib_copy(b):
-        at = pl.ds(b * half, half)
-        return remote(acts.at[:, at], acts_sib.at[:, at], sib_send.at[b + 1], sib_recv.at[b + 1], to_sib)
+        return remote(acts.at[:, pl.ds(edge + b * half, half)],
+                      acts.at[:, pl.ds(edge + rows + b * half, half)], sib_send.at[b + 1], sib_recv.at[b + 1], to_sib)
 
     for b in range(batch - 1):
         activate(b)
@@ -127,33 +127,34 @@
         return jnp.where(spot == half - 1, tail[batch + b : batch + b + 1, :],
                          pltpu.roll(block, half - 1, 0))
 
+    shifted = ([], [], [])
     for b in range(batch):
         g0 = 0.5 * g_ref[b].astype(f32)
         gext[pl.ds(b * half, half), :] = g0.astype(bf16)
-        for s, shifted in enumerate((sooner(g0, b, hg), g0, later(g0, b, hg))):
-            turned = shifted.T.astype(bf16)
-            for o in range(n):
-                gt[o % 2, s, b, o // 2] = turned[o * oblk : (o + 1) * oblk, :]
-    send_gt = remote(gt.at[1 - core], gt_sib, sib_send.at[0], sib_recv.at[0], to_sib)
+        for s, block in enumerate((sooner(g0, b, hg), g0, later(g0, b, hg))):
+            shifted[s].append(block)
+    for s in range(3):
+        turned = jnp.concatenate(shifted[s], axis=0).T.astype(bf16)
+        for m in range(chips):
+            low = turned[2 * m * oblk : (2 * m + 1) * oblk, :]
+            high = turned[(2 * m + 1) * oblk : (2 * m + 2) * oblk, :]
+            gt_all[s, m * oblk : (m + 1) * oblk, 0:rows] = jnp.where(core == 0, low, high)
+            gt_out[s, m * oblk : (m + 1) * oblk, :] = jnp.where(core == 0, high, low)
+    send_gt = remote(gt_out, gt_all.at[:, :, pl.ds(rows, rows)], sib_send.at[0], sib_recv.at[0], to_sib)
     send_gt.start()
     activate(batch - 1)
     sib_copy(batch - 1).start()
     for p in range(2):
         act, _ = phases(edge_rows(halo_f, edge - 2 + p, p))
-        acts[p, pl.ds(rows, edge), :] = act.astype(bf16)
+        acts[p, pl.ds(0, edge), :] = act.astype(bf16)
     send_gt.wait_recv()
     for b in range(batch):
         sib_copy(b).wait_recv()
 
     def product(s, p, slot):
+        total = jnp.dot(gt_all[s], acts[p, edge : edge + 2 * rows, :], preferred_element_type=f32)
         for m in range(chips):
-            total = jnp.zeros((oblk, chans), f32)
-            for b in range(batch):
-                total += jnp.dot(gt[core, s, b, m], acts[p, b * half : (b + 1) * half, :],
-                                 preferred_element_type=f32)
-                total += jnp.dot(gt_sib[s, b, m], acts_sib[p, b * half : (b + 1) * half, :],
-                                 preferred_element_type=f32)
-            prod[slot, m] = total
+            prod[slot, m] = total[m * oblk : (m + 1) * oblk, :]
 
     square = chips == 4
     hblk = oblk // 2
@@ -217,36 +218,39 @@
         w = [w_ref[k, :, pl.ds(c0, cols)] for k in range(taps)]
 
         def dots(pairs):
-            return sum(jnp.dot(acts[p], w[k], preferred_element_type=f32) for p, k in pairs)
+            total = None
+            for p, k in pairs:
+                one = jnp.dot(acts[p, 0 : edge + rows, :], w[k], preferred_element_type=f32)
+                total = one if total is None else total + one
+            return total
 
         before = dots(((0, 0), (1, 0), (1, 1)))
         middle = dots(((0, 1), (0, 2), (1, 2), (1, 3)))
         after = dots(((0, 3), (0, 4), (1, 4)))
         for b in range(batch):
-            at = slice(b * half, (b + 1) * half)
-            total = middle[at] + later(before[at], b, before[rows:]) + sooner(after[at], b, after[rows:])
+            at = slice(edge + b * half, edge + (b + 1) * half)
+            total = middle[at] + later(before[at], b, before[:edge]) + sooner(after[at], b, after[:edge])
             total += fd[b, :, pl.ds(c0, cols)].astype(f32)
             total += fd[b, :, pl.ds(chans + c0, cols)].astype(f32)
-            pooled[b, :, pl.ds(c0, cols)] = 0.5 * total
+            pooled[b * half : (b + 1) * half, pl.ds(c0, cols)] = 0.5 * total
         forward(tile)
 
     tiles = chans // cols
     for t in range(tiles + 1, taps):
         tap(t)
 
-    for b in range(batch):
-        whole = pooled[b]
-        for o in range(n):
-            tpart[o, b] = whole[:, o * oblk : (o + 1) * oblk].astype(bf16)
+    turned = pooled[...].T.astype(bf16)
+    for o in range(n):
+        tpart[o] = turned[o * oblk : (o + 1) * oblk, :]
 
     def t_copy(d):
         other = lax.rem(me + d, n)
-        return remote(tpart.at[other], trunk_ref.at[:, pl.ds(pl.multiple_of(me * half, edge), half)],
+        return remote(tpart.at[other], tland.at[me],
                       t_send.at[d - 1], t_recv.at[d - 1], {"seq": other})
 
     for d in range(1, n):
         t_copy(d).start()
-    trunk_ref[:, pl.ds(pl.multiple_of(me * half, edge), half), :] = tpart[me]
+    tland[me] = tpart[me]
 
     def z_copy(t, d):
         other = lax.rem(zme + d, zs)
@@ -315,6 +319,12 @@
     def _(t):
         collect(t)
 
+    for d in range(1, n):
+        t_copy(d).wait()
+    for o in range(n):
+        for b in range(batch):
+            trunk_ref[b, :, o * half : (o + 1) * half] = tland[o, :, b * half : (b + 1) * half]
+
     @pl.loop(0, taps)
     def _(t):
         total = zown[t, zme]
@@ -331,8 +341,6 @@
             for h in range(2):
                 y_copy(t, h).wait_send()
 
-    for d in range(1, n):
-        t_copy(d).wait()
     for b in range(batch):
         sib_copy(b).wait_send()
     send_gt.wait_send()
@@ -359,7 +367,7 @@
     trunk, igrad, wg = pl.pallas_call(
         functools.partial(kernel, n, zs),
         out_shape=(
-            jax.ShapeDtypeStruct((batch, half * n, oblk), bf16),
+            jax.ShapeDtypeStruct((batch, oblk, half * n), bf16),
             jax.ShapeDtypeStruct((batch, length, chans), bf16),
             jax.ShapeDtypeStruct((taps, oblk, iblk), f32),
         ),
@@ -371,11 +379,10 @@
             pltpu.VMEM((chans // 128, 64, 128), f32),
             pltpu.VMEM((2, batch, edge, chans), bf16),
             pltpu.VMEM((2, batch, edge, chans), bf16),
-            pltpu.VMEM((2, rows + edge, chans), bf16),
-            pltpu.VMEM((2, rows, chans), bf16),
+            pltpu.VMEM((2, edge + 2 * rows, chans), bf16),
             pltpu.VMEM((rows + edge, chans), bf16),
-            pltpu.VMEM((2, 3, batch, chips, oblk, half), bf16),
-            pltpu.VMEM((3, batch, chips, oblk, half), bf16),
+            pltpu.VMEM((3, chips * oblk, 2 * rows), bf16),
+            pltpu.VMEM((3, chips * oblk, rows), bf16),
             pltpu.VMEM((batch, half, 2 * chans), f32),
             pltpu.VMEM((2, chips, oblk, chans), f32),
             pltpu.VMEM(sends, bf16),
@@ -387,8 +394,9 @@
             pltpu.VMEM((taps, zs, oblk, iblk), bf16),
             pltpu.VMEM((taps, zs - 1, oblk, iblk), bf16),
             pltpu.VMEM((taps, zs, oblk, iblk), f32),
-            pltpu.VMEM((batch, half, chans), f32),
-            pltpu.VMEM((n, batch, half, oblk), bf16),
+            pltpu.VMEM((rows, chans), f32),
+            pltpu.VMEM((n, oblk, rows), bf16),
+            pltpu.VMEM((n, oblk, rows), bf16),
             dma((1,)), dma((4,)), dma((4,)), dma((batch + 1,)), dma((batch + 1,)),
             dma((taps, firsts)), dma((taps, firsts)), dma((taps, 2)), dma((taps, 2)),
             dma((taps, zs - 1)), dma((taps, zs - 1)),
@@ -401,7 +409,7 @@
             flops=2 * rows * chans * chans * 21, bytes_accessed=12_000_000, transcendentals=4 * rows * chans
         ),
     )(features, weight, cotangent)
-    return trunk, igrad, jnp.swapaxes(wg, 1, 2)
+    return jnp.swapaxes(trunk, 1, 2), igrad, jnp.swapaxes(wg, 1, 2)
 
 
 def solution(mesh):

time: 66.2 us -> 64.7 us (0.977)
  Pallas kernels: 61 us -> 58.7 us
  local copies, waits for them, and re-layouts: 4.36 us -> 5.06 us
    pallas_call x1, Pallas kernels: 61 us -> 58.7 us  [shards(): pl.pallas_call(functools.partial(kernel, n, zs), out_shape=(jax.ShapeDtyp...]
    unnamed x7 -> x5, local copies, waits for them, and re-layouts: 4.36 us -> 5.06 us
where the time goes in v3:
time: 64.7 us; the launch traced here: 64.5 us
  Pallas kernels  58.7 us (91%)
  local copies, waits for them, and re-layouts  5.06 us (8%)
  between operations  0.65 us (1%)
    pallas_call x1, Pallas kernels, shards(): pl.pallas_call(functools.partial(kernel, n, zs), out_shape=(jax.ShapeDtyp...  58.7 us
    unnamed x5, local copies, waits for them, and re-layouts  5.06 us

profile of v3, /device:TPU:0, one launch (start us, length us, event | category | flops | bytes accessed | tf_op | source)
XLA Modules:
  0.0 64.5 jit_solution(3438877190914545752)
XLA Ops:
  0.6 58.7 %shard_map.58 = (bf16[2,96,1536]{2,1,0:T(8,128)(2,1)}, bf16[2,384,768]{2,1,0:T(8,128)(2,1)}, f32[5,96,192]{2,1,0:T(8,128)}) custom-call(bf16[2,384,768]{2,1,0:T(8,128)(2,1)} %f_ref.1, bf16[5,768,768]{2,1,0:T(8,128)(2,1)} %w_hbm.1, bf16[2,192,768]{2,1,0:T(8,128)(2,1)} %g_ref.1), custom_call_target="tpu_custom_call" | custom-call | flops 9512681472 | bytes 12000000 | tf_op jit(solution)/shard_map/pallas_call | solution.py:367
  59.4 0.0 copy-start
  59.4 2.1 %copy.6 = f32[5,192,96]{2,1,0:T(8,128)} copy(f32[5,192,96]{1,2,0:T(8,128)} %bitcast.3) | data formatting | bytes 737280
  61.5 1.9 %copy.9 = bf16[2,1536,96]{1,2,0:T(8,128)(2,1)} copy(bf16[2,1536,96]{1,2,0:T(8,128)(2,1)} %bitcast.2) | data formatting | bytes 1179648
  63.4 0.0 copy-done
  63.4 1.0 %copy.10 = bf16[2,384,768]{2,1,0:T(8,128)(2,1)} copy(bf16[2,384,768]{2,1,0:T(8,128)(2,1)S(1)} %copy-done) | data formatting | bytes 2359296
Async XLA Ops:
  59.4 4.1 %copy-start = (bf16[2,384,768]{2,1,0:T(8,128)(2,1)S(1)}, bf16[2,384,768]{2,1,0:T(8,128)(2,1)}, u32[]{:S(2)}) copy-start(bf16[2,384,768]{2,1,0:T(8,128)(2,1)} %get-tuple-element.16) | copy-start | bytes 3538948

commit v4 on v3

--- a/solution.py
+++ b/solution.py
@@ -52,7 +52,6 @@
     for d in range(1, zs):
         pl.semaphore_signal(barrier, inc=1, device_id={"dp": lax.rem(zme + d, zs)},
                             device_id_type=pl.DeviceIdType.MESH)
-    pl.semaphore_wait(barrier, n - 1 + zs - 1)
 
     def remote(src, dst, ssem, rsem, where):
         return pltpu.make_async_remote_copy(
@@ -69,8 +68,6 @@
                             halo_send.at[2 * side], halo_recv.at[2 * side], where))
         halos.append(remote(g_ref.at[:, pl.ds(start, edge)], halo_g.at[side],
                             halo_send.at[2 * side + 1], halo_recv.at[2 * side + 1], where))
-    for copy in halos:
-        copy.start()
 
     chunk = 32
     per = half // chunk
@@ -96,7 +93,12 @@
         return remote(acts.at[:, pl.ds(edge + b * half, half)],
                       acts.at[:, pl.ds(edge + rows + b * half, half)], sib_send.at[b + 1], sib_recv.at[b + 1], to_sib)
 
-    for b in range(batch - 1):
+    activate(0)
+    pl.semaphore_wait(barrier, n - 1 + zs - 1)
+    for copy in halos:
+        copy.start()
+    sib_copy(0).start()
+    for b in range(1, batch):
         activate(b)
         sib_copy(b).start()
 
@@ -142,8 +144,6 @@
             gt_out[s, m * oblk : (m + 1) * oblk, :] = jnp.where(core == 0, high, low)
     send_gt = remote(gt_out, gt_all.at[:, :, pl.ds(rows, rows)], sib_send.at[0], sib_recv.at[0], to_sib)
     send_gt.start()
-    activate(batch - 1)
-    sib_copy(batch - 1).start()
     for p in range(2):
         act, _ = phases(edge_rows(halo_f, edge - 2 + p, p))
         acts[p, pl.ds(0, edge), :] = act.astype(bf16)
@@ -332,7 +332,7 @@
             z_copy(t, d).wait_recv()
         for d in range(1, zs):
             total += zrecv[t, d - 1].astype(f32)
-        wg_ref[t] = total
+        wg_ref[t] = total.T
         for d in range(1, zs):
             z_copy(t, d).wait_send()
         for d in range(firsts):
@@ -369,7 +369,7 @@
         out_shape=(
             jax.ShapeDtypeStruct((batch, oblk, half * n), bf16),
             jax.ShapeDtypeStruct((batch, length, chans), bf16),
-            jax.ShapeDtypeStruct((taps, oblk, iblk), f32),
+            jax.ShapeDtypeStruct((taps, iblk, oblk), f32),
         ),
         in_specs=[vmem, pl.BlockSpec(memory_space=pl.ANY), vmem],
         out_specs=(vmem,) * 3,
@@ -409,7 +409,7 @@
             flops=2 * rows * chans * chans * 21, bytes_accessed=12_000_000, transcendentals=4 * rows * chans
         ),
     )(features, weight, cotangent)
-    return jnp.swapaxes(trunk, 1, 2), igrad, jnp.swapaxes(wg, 1, 2)
+    return jnp.swapaxes(trunk, 1, 2), igrad, wg
 
 
 def solution(mesh):

time: 64.7 us -> 63.2 us (0.977)
  local copies, waits for them, and re-layouts: 5.06 us -> 4.16 us
    unnamed x5 -> x7, local copies, waits for them, and re-layouts: 5.06 us -> 4.16 us
where the time goes in v4:
time: 63.2 us; the launch traced here: 62.9 us
  Pallas kernels  58.1 us (92%)
  local copies, waits for them, and re-layouts  4.16 us (7%)
  between operations  0.65 us (1%)
    pallas_call x1, Pallas kernels, shards(): pl.pallas_call(functools.partial(kernel, n, zs), out_shape=(jax.ShapeDtyp...  58.1 us
    unnamed x7, local copies, waits for them, and re-layouts  4.16 us

profile of v4, /device:TPU:0, one launch (start us, length us, event | category | flops | bytes accessed | tf_op | source)
XLA Modules:
  0.0 62.9 jit_solution(505081314963276936)
XLA Ops:
  0.6 58.1 %shard_map.58 = (bf16[2,96,1536]{2,1,0:T(8,128)(2,1)}, bf16[2,384,768]{2,1,0:T(8,128)(2,1)}, f32[5,192,96]{2,1,0:T(8,128)}) custom-call(bf16[2,384,768]{2,1,0:T(8,128)(2,1)} %f_ref.1, bf16[5,768,768]{2,1,0:T(8,128)(2,1)} %w_hbm.1, bf16[2,192,768]{2,1,0:T(8,128)(2,1)} %g_ref.1), custom_call_target="tpu_custom_call" | custom-call | flops 9512681472 | bytes 12000000 | tf_op jit(solution)/shard_map/pallas_call | solution.py:367
  58.8 0.0 copy-start
  58.8 2.0 %copy.9 = bf16[2,1536,96]{1,2,0:T(8,128)(2,1)} copy(bf16[2,1536,96]{1,2,0:T(8,128)(2,1)} %bitcast.1) | data formatting | bytes 1179648
  60.8 0.0 copy-done
  60.8 0.0 copy-start.1
  60.8 1.0 %copy.10 = bf16[2,384,768]{2,1,0:T(8,128)(2,1)} copy(bf16[2,384,768]{2,1,0:T(8,128)(2,1)S(1)} %copy-done) | data formatting | bytes 2359296
  61.8 0.3 copy-done.1
  62.2 0.8 %copy.11 = f32[5,192,96]{2,1,0:T(8,128)} copy(f32[5,192,96]{2,1,0:T(8,128)S(1)} %copy-done.1) | data formatting | bytes 737280
Async XLA Ops:
  58.8 2.0 %copy-start = (bf16[2,384,768]{2,1,0:T(8,128)(2,1)S(1)}, bf16[2,384,768]{2,1,0:T(8,128)(2,1)}, u32[]{:S(2)}) copy-start(bf16[2,384,768]{2,1,0:T(8,128)(2,1)} %get-tuple-element.13) | copy-start | bytes 3538948
  60.8 1.4 %copy-start.1 = (f32[5,192,96]{2,1,0:T(8,128)S(1)}, f32[5,192,96]{2,1,0:T(8,128)}, u32[]{:S(2)}) copy-start(f32[5,192,96]{2,1,0:T(8,128)} %get-tuple-element.14) | copy-start | bytes 1105924
